TPU v7x, 32 devices: a whole 2x2x4 slice. The times are simulated.
32 devices in a mesh: groups: 1, ep: 16 (over z, y, x), wr: 2 (over core).
Axes of the slice: x: 2, y: 2, z: 4, core: 2. Of those that a mesh axis runs over, the one named last changes fastest.
Arguments:
- hidden: bfloat16 [2048, 8, 1024], P(('groups', 'ep'), None, 'wr'), may hold values from -6 to 6
- weight: bfloat16 [16, 1024, 3584], P('ep', None, 'wr'), may hold values from -0.1875 to 0.1875
- expert_ids: int32 [2048, 8], P(('groups', 'ep')), may hold values from 0 to 15, all different within a row; in each aligned block of 64 rows (0 to 63, 64 to 127, ...) at most 40 rows name the same one
- gate_score: int32 [2048, 8], P(('groups', 'ep')), may hold values from 1 to 64
Outputs:
- mixed: bfloat16 [2048, 3584], P(('groups', 'ep'), 'wr')
Inputs may be any that keep to these rules, and one draw needn't show every extreme that they name: `expert_ids`: each token names 8 different experts; in each aligned block of 64 tokens no expert is named by more than 40 tokens, and in every draw some block has an expert named by exactly 40 tokens.
All inputs are finite; a program needn't handle non-finite values.
Results may differ from a plain program's by a relative error of at most 0.0049.
Values may be sent and summed in bfloat16 or wider, within the bound.
A program may use at most 64 MiB of HBM per device.

v0:
```python
import jax
import jax.numpy as jnp
from jax import lax
from jax.sharding import PartitionSpec as P


def mixing(gate_score):
    score = gate_score.astype(jnp.float32)
    return 2.827 * score / jnp.sum(score, axis=1, keepdims=True)


def slot_numbers(ids_flat, experts, block_pairs):
    onehot = (ids_flat[:, None] == jnp.arange(experts, dtype=jnp.int32)[None, :]).astype(jnp.int32)
    grouped = onehot.reshape(-1, block_pairs, experts)
    before = jnp.cumsum(grouped, axis=1) - grouped
    return jnp.sum(before * grouped, axis=2).reshape(-1)


def per_device(hidden, weight, expert_ids, gate_score):
    tok_dev, top, part_width = hidden.shape
    experts = lax.axis_size("ep")
    half = tok_dev // 2
    cap = max(2, 5 * half * top // (4 * experts))
    side = lax.axis_index("wr")
    gates = mixing(gate_score)
    local_weight = weight[0]
    source = lax.all_gather(hidden, "wr", axis=2, tiled=True)
    start = side * half
    mine = lax.dynamic_slice_in_dim(source, start, half, 0)
    my_ids = lax.dynamic_slice_in_dim(expert_ids, start, half, 0).reshape(-1)
    my_gates = lax.dynamic_slice_in_dim(gates, start, half, 0)
    slot = slot_numbers(my_ids, experts, half * top)
    target = my_ids * cap + slot
    row_width = mine.shape[2]
    outgoing = (
        jnp.zeros((experts * cap, row_width), jnp.bfloat16)
        .at[target]
        .set(mine.reshape(half * top, row_width))
    )
    outgoing = outgoing.reshape(experts, cap, row_width)
    received = lax.all_to_all(outgoing, "ep", split_axis=0, concat_axis=0, tiled=True)
    result = jnp.einsum(
        "scj,jd->scd",
        received,
        lax.all_gather(local_weight, "wr", axis=1, tiled=True),
        preferred_element_type=jnp.float32,
    ).astype(jnp.bfloat16)
    returned = lax.all_to_all(result, "ep", split_axis=0, concat_axis=0, tiled=True)
    full_width = returned.shape[2]
    picked = returned.reshape(experts * cap, full_width)[target]
    weighted = picked.astype(jnp.float32).reshape(half, top, full_width) * my_gates[:, :, None]
    partial_out = jnp.sum(weighted, axis=1).astype(jnp.bfloat16)
    return lax.all_to_all(partial_out, "wr", split_axis=1, concat_axis=0, tiled=True)


def solution(mesh):
    in_specs = (
        P(("groups", "ep"), None, "wr"),
        P("ep", None, "wr"),
        P(("groups", "ep"), None),
        P(("groups", "ep"), None),
    )
    out_specs = P(("groups", "ep"), "wr")
    return jax.shard_map(
        per_device, mesh=mesh, in_specs=in_specs, out_specs=out_specs, check_vma=False
    )
```

profile of v0, /device:TPU:14, one launch (start us, length us, event | category | flops | bytes accessed | tf_op | source)
XLA Modules:
  0.0 206.6 jit_solution(9241931432012037776)
XLA Ops:
  6.5 0.7 all-gather.4.cloned.1.call-update
  7.3 0.7 all-gather.6.cloned.1.call-update
  8.0 0.1 broadcast_multiply_fusion
  8.1 0.1 copy.20
  8.2 0.1 eq.25
  8.3 1.2 reduce-window.6
  9.5 0.2 slice_reduce_fusion
  9.8 0.1 copy.23
  9.8 0.1 copy.19
  9.9 0.1 mul.39
  10.0 0.1 broadcast.69
  10.1 0.1 fusion.10
  10.2 10.7 %all-gather.4.cloned.1.call-done = bf16[128,8,1024]{2,1,0:T(8,128)(2,1)} async-done(((bf16[128,8,512]{2,1,0:T(8,128)(2,1)}), bf16[128,8,1024]{2,1,0:T(8,128)(2,1)}) %all-gather.4.cloned.1.call-update) | async-done | bytes 2097168 | tf_op jit(solution)/shard_map/all_gather | solution.py:27
  20.9 3.6 %scatter_custom_fusion = bf16[640,1024]{1,0:T(8,128)(2,1)S(1)} fusion(s32[512]{0:T(512)S(1)} %bitcast.45, bf16[128,8,1024]{2,1,0:T(8,128)(2,1)} %all-gather.4.cloned.1.call-done, s32[]{:T(128)S(6)} %select_n.16, s32[]{:T(128)} %constant.4.clone.1, bf16[]{:T(256)} %constant.9.clone.1), kind=kCustom, calls=%fused_computation.7 | custom fusion | bytes 2360324 | tf_op jit(solution)/shard_map/scatter | solution.py:38
  24.5 37.1 %all_to_all.26 = bf16[16,40,1024]{2,1,0:T(8,128)(2,1)S(1)} all-to-all(bf16[16,40,1024]{2,1,0:T(8,128)(2,1)S(1)} %bitcast.38), channel_id=1, replica_groups=mesh['groups'=1,'ep'=16,'wr'=2] {'ep'}, dimensions={0} | all-to-all | bytes 2621440 | tf_op jit(solution)/shard_map/all_to_all | solution.py:41
  61.5 9.6 %fusion.3 = bf16[16,40,3584]{2,1,0:T(8,128)(2,1)} fusion(bf16[16,40,1024]{2,1,0:T(8,128)(2,1)S(1)} %all_to_all.26, bf16[1,1024,3584]{2,1,0:T(8,128)(2,1)} %all-gather.6.cloned.1.call-done), kind=kOutput, calls=%fused_computation.6 | convolution fusion | flops 4699914240 | bytes 13238272 | tf_op jit(solution)/shard_map/scj,jd->scd/dot_general | solution.py:42
  71.2 7.2 %all-to-all-start.1 = ((bf16[16,40,3584]{2,1,0:T(8,128)(2,1)}), bf16[16,40,3584]{2,1,0:T(8,128)(2,1)}, u32[]{:S(2)}, u32[]{:S(2)}) async-start(bf16[16,40,3584]{2,1,0:T(8,128)(2,1)} %fusion.3), calls=%async_computation.1 | async-start | bytes 9175040 | tf_op jit(solution)/shard_map/all_to_all | solution.py:48
  78.4 0.1 constant_dynamic-slice_fusion
  78.5 0.1 copy.24
  78.5 100.5 %all-to-all-done.1 = bf16[16,40,3584]{2,1,0:T(8,128)(2,1)} async-done(((bf16[16,40,3584]{2,1,0:T(8,128)(2,1)}), bf16[16,40,3584]{2,1,0:T(8,128)(2,1)}, u32[]{:S(2)}, u32[]{:S(2)}) %all-to-all-start.1) | async-done | bytes 4587552 | tf_op jit(solution)/shard_map/all_to_all | solution.py:48
  179.0 10.8 %gather_fusion = bf16[512,3584]{1,0:T(8,128)(2,1)} fusion(bf16[640,3584]{1,0:T(8,128)(2,1)} %bitcast.12, s32[1024]{0:T(1024)S(1)} %pad_clamp_fusion), kind=kCustom, calls=%fused_computation | custom fusion | bytes 7342080 | tf_op jit(solution)/shard_map/gather | solution.py:50
  189.8 5.1 %fusion = bf16[64,3584]{1,0:T(8,128)(2,1)S(1)} fusion(bf16[512,3584]{1,0:T(8,128)(2,1)} %gather_fusion, f32[64,8]{1,0:T(8,128)S(1)} %copy.24), kind=kLoop, calls=%fused_computation.3 | loop fusion | flops 5275648 | bytes 4130816 | tf_op jit(solution)/shard_map/reduce_sum | solution.py:52
  194.9 4.1 %all_to_all.27 = bf16[64,2,1792]{2,0,1:T(8,128)(2,1)S(1)} all-to-all(bf16[64,2,1792]{2,0,1:T(8,128)(2,1)S(1)} %bitcast.39), channel_id=1, replica_groups=mesh['groups'=1,'ep'=16,'wr'=2] {'wr'}, dimensions={1} | all-to-all | bytes 917504 | tf_op jit(solution)/shard_map/all_to_all | solution.py:53
  199.0 0.8 copy.30
  (17 shorter events, 0.2 us)
Async XLA Ops:
  6.5 1.5 copy-start.1
  6.5 14.3 %all-gather.4.cloned.1.call-start = ((), (), s32[]{:S(2)}) async-start(), calls=%async_computation.3 | async-start | bytes 3145728 | tf_op jit(solution)/shard_map/all_gather | solution.py:27
  7.3 54.3 %all-gather.6.cloned.1.call-start = ((), (), s32[]{:S(2)}) async-start(), calls=%async_computation.4 | async-start | bytes 11010048 | tf_op jit(solution)/shard_map/all_gather | solution.py:45
  71.2 7.2 %copy-start = (s32[128,8]{0,1:T(8,128)S(1)}, s32[128,8]{0,1:T(8,128)}, u32[]{:S(2)}) copy-start(s32[128,8]{0,1:T(8,128)} %param.7) | copy-start | bytes 12292
  71.2 107.9 %all-to-all-start.1 = ((bf16[16,40,3584]{2,1,0:T(8,128)(2,1)}), bf16[16,40,3584]{2,1,0:T(8,128)(2,1)}, u32[]{:S(2)}, u32[]{:S(2)}) async-start(bf16[16,40,3584]{2,1,0:T(8,128)(2,1)} %fusion.3), calls=%async_computation.1 | async-start | bytes 9175040 | tf_op jit(solution)/shard_map/all_to_all | solution.py:48
Sparse Core Ops, SparseCore 0:
  8.9 11.9 all-gather.3
  22.4 19.4 all-gather.5
where the time goes:
time: 207 us
  waiting for transfers between devices  113 us (55%)
  blocking collectives  41.2 us (20%)
  local copies, waits for them, and re-layouts  16.1 us (8%)
  between operations  13.5 us (7%)
  matrix products  9.6 us (5%)
  starting transfers between devices  7.23 us (3%)
  other arithmetic  6.48 us (3%)
    all_to_all x1, waiting for transfers between devices, per_device(): lax.all_to_all(result, 'ep', split_axis=0, concat_axis=0, tiled=True)  100 us
    all_to_all x1, blocking collectives, per_device(): lax.all_to_all(outgoing, 'ep', split_axis=0, concat_axis=0, tiled=True)  37.1 us
    gather x1, local copies, waits for them, and re-layouts, per_device(): picked = returned.reshape(experts * cap, full_width)[target]  10.8 us
    all_gather x1, waiting for transfers between devices, per_device(): source = lax.all_gather(hidden, 'wr', axis=2, tiled=True)  10.7 us
    dot_general x1, matrix products, per_device(): jnp.einsum('scj,jd->scd', received, lax.all_gather(local_weight, 'wr', ax...  9.6 us
    all_to_all x1, starting transfers between devices, per_device(): lax.all_to_all(result, 'ep', split_axis=0, concat_axis=0, tiled=True)  7.19 us
    reduce_sum x1, other arithmetic, per_device(): partial_out = jnp.sum(weighted, axis=1).astype(jnp.bfloat16)  5.06 us
  transfers between devices with their start and end apart: 3, of which 2 were waited for; matrix products, arithmetic and copies ran while one was open for 3% of the time, Pallas kernels for 0%

commit v1 on v0

--- a/solution.py
+++ b/solution.py
@@ -1,7 +1,238 @@
+import functools
+
 import jax
 import jax.numpy as jnp
 from jax import lax
+from jax.experimental import pallas as pl
+from jax.experimental.pallas import tpu as pltpu
 from jax.sharding import PartitionSpec as P
+
+MESH = pl.DeviceIdType.MESH
+ORDER = (3, 1, 2, 0)
+EMPTY = 255.0
+TILE = 256
+
+
+def partner(index, step):
+    if step == 0:
+        return index
+    if step == 1:
+        return index + 1 - 2 * (index % 2)
+    if step == 2:
+        return index + 2 - 4 * (index // 2)
+    return 3 - index
+
+
+def iota(shape, axis):
+    return lax.broadcasted_iota(jnp.int32, shape, axis)
+
+
+def onehot(condition):
+    return condition.astype(jnp.float32).astype(jnp.bfloat16)
+
+
+def mm(a, b):
+    return jnp.dot(a, b, preferred_element_type=jnp.float32)
+
+
+def kernel(rows, ids_ref, score_ref, flat_ref, hidden_ref, weight_hbm, out_ref,
+           weight, outgoing, arrived, result, planar, table, zsend, zrecv,
+           wsem, d_send, d_recv, f_send, f_recv, p_send, p_recv,
+           t_send, t_recv, z_send, z_recv):
+    me, w = lax.axis_index("ep"), lax.axis_index("wr")
+    zm, pm = me // 4, me % 4
+    tokens, top = ids_ref.shape
+    pairs, part = hidden_ref.shape
+    group = 4 * rows
+    width = out_ref.shape[1]
+
+    load = pltpu.make_async_copy(weight_hbm, weight, wsem)
+    load.start()
+
+    barrier = pltpu.get_barrier_semaphore()
+    for j in range(4):
+        for q in range(4):
+            if j or q:
+                pl.semaphore_signal(
+                    barrier, inc=1, device_id_type=MESH,
+                    device_id={"ep": partner(zm, j) * 4 + partner(pm, q), "wr": w})
+    pl.semaphore_signal(barrier, inc=1, device_id_type=MESH, device_id={"ep": me, "wr": 1 - w})
+
+    flat = flat_ref[...]
+    named = onehot(flat == iota((16, pairs), 0))
+    earlier = onehot(iota((pairs, pairs), 0) < iota((pairs, pairs), 1))
+    slot = jnp.sum(mm(named, earlier) * named.astype(jnp.float32), axis=0, keepdims=True)
+    target = flat * rows + slot.astype(jnp.int32)
+
+    def block(ref, j, p):
+        return ref.at[j, pl.ds(pl.multiple_of(p * rows, 16), rows)]
+
+    pl.semaphore_wait(barrier, 16)
+
+    dispatch = {}
+    for j in ORDER:
+        zd = partner(zm, j)
+        pick = onehot(target - zd * group == iota((group, pairs), 0))
+        outgoing[j] = mm(pick, hidden_ref[...]).astype(jnp.bfloat16)
+        for q in range(4):
+            pd = partner(pm, q)
+            if j == 0 and q == 0:
+                arrived[w, 0, pl.ds(pl.multiple_of(pm * rows, 16), rows)] = (
+                    outgoing[0, pl.ds(pl.multiple_of(pm * rows, 16), rows)])
+                continue
+            copy = pltpu.make_async_remote_copy(
+                src_ref=block(outgoing, j, pd),
+                dst_ref=arrived.at[w, j, pl.ds(pl.multiple_of(pm * rows, 16), rows)],
+                send_sem=d_send.at[j, q], recv_sem=d_recv.at[j, q],
+                device_id={"ep": zd * 4 + pd, "wr": w}, device_id_type=MESH)
+            copy.start()
+            dispatch[j, q] = copy
+
+    ids, score = ids_ref[...], score_ref[...]
+    lane = iota((tokens, 16), 1)
+    scores = jnp.zeros((tokens, 16), jnp.float32)
+    for k in range(top):
+        scores = scores + jnp.where(
+            ids[:, k:k + 1] == lane, score[:, k:k + 1].astype(jnp.float32), 0.0)
+    gates = 2.827 * scores / jnp.sum(scores, axis=1, keepdims=True)
+    before = mm(onehot(iota((tokens, tokens), 1) < iota((tokens, tokens), 0)), onehot(scores > 0))
+    place = jnp.where(scores > 0, before, EMPTY).astype(jnp.bfloat16)
+    high = gates.astype(jnp.bfloat16)
+    low = (gates - high.astype(jnp.float32)).astype(jnp.bfloat16)
+
+    def put(values, shift):
+        return mm(values, onehot(iota((16, 128), 0) + shift == iota((16, 128), 1)))
+
+    table[0] = (put(place, 0) + put(high, 16) + put(low, 32)).astype(jnp.bfloat16)
+    tables = {}
+    for j in range(1, 4):
+        tables[j] = pltpu.make_async_remote_copy(
+            src_ref=table.at[0], dst_ref=table.at[j],
+            send_sem=t_send.at[j], recv_sem=t_recv.at[j],
+            device_id={"ep": partner(zm, j) * 4 + pm, "wr": w}, device_id_type=MESH)
+        tables[j].start()
+
+    planars, forwards, zcopies = {}, {}, {}
+
+    def forward(j):
+        for q in range(4):
+            if j or q:
+                dispatch[j, q].wait_recv()
+        forwards[j] = pltpu.make_async_remote_copy(
+            src_ref=arrived.at[w, j], dst_ref=arrived.at[w, j],
+            send_sem=f_send.at[j], recv_sem=f_recv.at[j],
+            device_id={"ep": me, "wr": 1 - w}, device_id_type=MESH)
+        forwards[j].start()
+
+    def expert(j):
+        forwards[j].wait_recv()
+
+        @pl.loop(0, width // TILE)
+        def _(i):
+            cols = pl.ds(pl.multiple_of(i * TILE, TILE), TILE)
+            total = mm(arrived[0, j], weight[:part, cols]) + mm(arrived[1, j], weight[part:, cols])
+            result[j, :, cols] = total.astype(jnp.bfloat16)
+
+        for q in range(1, 4):
+            pd = partner(pm, q)
+            planars[j, q] = pltpu.make_async_remote_copy(
+                src_ref=block(result, j, pd), dst_ref=block(planar, j, pm),
+                send_sem=p_send.at[j, q], recv_sem=p_recv.at[j, q],
+                device_id={"ep": zm * 4 + pd, "wr": w}, device_id_type=MESH)
+            planars[j, q].start()
+        own = pl.ds(pl.multiple_of(pm * rows, 16), rows)
+        planar[j, own] = result[j, own]
+
+    def combine(j):
+        if j:
+            tables[j].wait_recv()
+        info = table[j]
+        column = iota((128, group), 1)
+        quarter = sum((column >= n * rows).astype(jnp.int32) for n in range(1, 4))
+        source = zm * 4 + quarter
+
+        def spread(shift):
+            return mm(info, onehot(iota((128, group), 0) == source + shift))
+
+        wide = iota((tokens, group), 1)
+        within = wide - rows * sum((wide >= n * rows).astype(jnp.int32) for n in range(1, 4))
+        hit = spread(0) == within.astype(jnp.float32)
+        high = jnp.where(hit, spread(16), 0.0).astype(jnp.bfloat16)
+        low = jnp.where(hit, spread(32), 0.0).astype(jnp.bfloat16)
+        for q in range(1, 4):
+            planars[j, q].wait_recv()
+        if j == 2:
+            zcopies[3].wait_recv()
+        if j == 0:
+            zcopies[1].wait_recv()
+            zcopies[2].wait_recv()
+
+        @pl.loop(0, width // TILE)
+        def _(i):
+            cols = pl.ds(pl.multiple_of(i * TILE, TILE), TILE)
+            values = planar[j, :, cols]
+            total = mm(high, values) + mm(low, values)
+            if j == 2:
+                total = total + zrecv[3, :, cols].astype(jnp.float32)
+            if j == 0:
+                total = (total + zrecv[1, :, cols].astype(jnp.float32)
+                         + zrecv[2, :, cols].astype(jnp.float32))
+                out_ref[:, cols] = total.astype(jnp.bfloat16)
+            else:
+                zsend[j, :, cols] = total.astype(jnp.bfloat16)
+
+        if j:
+            zcopies[j] = pltpu.make_async_remote_copy(
+                src_ref=zsend.at[j], dst_ref=zrecv.at[j],
+                send_sem=z_send.at[j], recv_sem=z_recv.at[j],
+                device_id={"ep": partner(zm, 2 if j == 2 else 1) * 4 + pm, "wr": w},
+                device_id_type=MESH)
+            zcopies[j].start()
+
+    load.wait()
+    for n, j in enumerate(ORDER):
+        forward(j)
+        expert(j)
+        if n:
+            combine(ORDER[n - 1])
+    combine(ORDER[-1])
+
+    for copies in (dispatch, tables, forwards, planars, zcopies):
+        for copy in copies.values():
+            copy.wait_send()
+
+
+def by_kernel(hidden, weight, expert_ids, gate_score):
+    tokens, top, part = hidden.shape
+    full, width = weight.shape[1:]
+    pairs = tokens * top
+    rows = 2 * (5 * pairs // 2 // (4 * 16))
+    group = 4 * rows
+    bf16 = jnp.bfloat16
+    vmem = pl.BlockSpec(memory_space=pltpu.VMEM)
+    dma = pltpu.SemaphoreType.DMA
+    return pl.pallas_call(
+        functools.partial(kernel, rows),
+        out_shape=jax.ShapeDtypeStruct((tokens, width), bf16),
+        in_specs=[vmem, vmem, vmem, vmem, pl.BlockSpec(memory_space=pl.ANY)],
+        out_specs=vmem,
+        scratch_shapes=[
+            pltpu.VMEM((full, width), bf16),
+            pltpu.VMEM((4, group, part), bf16),
+            pltpu.VMEM((2, 4, group, part), bf16),
+            pltpu.VMEM((4, group, width), bf16),
+            pltpu.VMEM((4, group, width), bf16),
+            pltpu.VMEM((4, tokens, 128), bf16),
+            pltpu.VMEM((4, tokens, width), bf16),
+            pltpu.VMEM((4, tokens, width), bf16),
+            dma, dma((4, 4)), dma((4, 4)), dma((4,)), dma((4,)), dma((4, 4)), dma((4, 4)),
+            dma((4,)), dma((4,)), dma((4,)), dma((4,)),
+        ],
+        compiler_params=pltpu.CompilerParams(
+            collective_id=0, has_side_effects=True, vmem_limit_bytes=50 * 1024 * 1024),
+        cost_estimate=pl.CostEstimate(
+            flops=2 * 16 * rows * full * width, bytes_accessed=2 * full * width, transcendentals=0),
+    )(expert_ids, gate_score, expert_ids.reshape(1, pairs), hidden.reshape(pairs, part), weight[0])
 
 
 def mixing(gate_score):
@@ -16,7 +247,7 @@
     return jnp.sum(before * grouped, axis=2).reshape(-1)
 
 
-def per_device(hidden, weight, expert_ids, gate_score):
+def by_collectives(hidden, weight, expert_ids, gate_score):
     tok_dev, top, part_width = hidden.shape
     experts = lax.axis_size("ep")
     half = tok_dev // 2
@@ -53,6 +284,12 @@
     return lax.all_to_all(partial_out, "wr", split_axis=1, concat_axis=0, tiled=True)
 
 
+def per_device(hidden, weight, expert_ids, gate_score):
+    if lax.axis_size("ep") == 16 and lax.axis_size("wr") == 2:
+        return by_kernel(hidden, weight, expert_ids, gate_score)
+    return by_collectives(hidden, weight, expert_ids, gate_score)
+
+
 def solution(mesh):
     in_specs = (
         P(("groups", "ep"), None, "wr"),

time: 207 us -> 95.8 us (0.46)
  the two profiles are of different devices: /device:TPU:14 before, /device:TPU:0 now
where the time goes in v1:
time: 95.8 us; the launch traced here: 95.6 us
  Pallas kernels  91.9 us (96%)
  local copies, waits for them, and re-layouts  3.66 us (4%)
    pallas_call x1, Pallas kernels, by_kernel(): pl.pallas_call(functools.partial(kernel, rows), out_shape=jax.ShapeDtypeS...  91.9 us
    unnamed x5, local copies, waits for them, and re-layouts  3.56 us

profile of v1, /device:TPU:0, one launch (start us, length us, event | category | flops | bytes accessed | tf_op | source)
XLA Modules:
  0.0 95.6 jit_solution(6781314016886859941)
XLA Ops:
  0.0 0.8 copy.9.ids_ref
  0.8 0.1 reshape.6.flat_ref
  0.9 0.8 copy.10.score_ref
  1.7 0.0 copy-start
  1.7 1.2 %copy-done = bf16[128,8,512]{2,1,0:T(8,128)(2,1)S(1)} copy-done((bf16[128,8,512]{2,1,0:T(8,128)(2,1)S(1)}, bf16[128,8,512]{2,1,0:T(8,128)(2,1)}, u32[]{:S(2)}) %copy-start) | copy-done | bytes 1048600
  2.9 91.9 %shard_map.46 = bf16[128,1792]{1,0:T(8,128)(2,1)S(1)} custom-call(s32[128,8]{1,0:T(8,128)S(1)} %copy.9.ids_ref, s32[128,8]{1,0:T(8,128)S(1)} %copy.10.score_ref, s32[1,1024]{1,0:T(1,128)S(1)} %reshape.6.flat_ref, bf16[1024,512]{1,0:T(8,128)(2,1)S(1)} %bitcast.2, bf16[1024,1792]{1,0:T(8,128)(2,1)} %bitcast.3), custom_call_target="tpu_custom_call" | custom-call | flops 4697620480 | bytes 3670016 | tf_op jit(solution)/shard_map/pallas_call | solution.py:214
  94.8 0.8 copy.12
Async XLA Ops:
  1.7 1.2 %copy-start = (bf16[128,8,512]{2,1,0:T(8,128)(2,1)S(1)}, bf16[128,8,512]{2,1,0:T(8,128)(2,1)}, u32[]{:S(2)}) copy-start(bf16[128,8,512]{2,1,0:T(8,128)(2,1)} %param.4) | copy-start | bytes 3145732

commit v2 on v1

--- a/solution.py
+++ b/solution.py
@@ -8,7 +8,8 @@
 from jax.sharding import PartitionSpec as P
 
 MESH = pl.DeviceIdType.MESH
-ORDER = (3, 1, 2, 0)
+ORDER = (1, 3, 2, 0)
+LAG = 2
 EMPTY = 255.0
 TILE = 256
 
@@ -35,17 +36,19 @@
     return jnp.dot(a, b, preferred_element_type=jnp.float32)
 
 
-def kernel(rows, ids_ref, score_ref, flat_ref, hidden_ref, weight_hbm, out_ref,
-           weight, outgoing, arrived, result, planar, table, zsend, zrecv,
-           wsem, d_send, d_recv, f_send, f_recv, p_send, p_recv,
+def kernel(rows, ids_ref, score_ref, hidden_hbm, weight_hbm, out_ref,
+           hidden_ref, weight, outgoing, arrived, result, planar, table, mixer, zsend, zrecv,
+           hsem, wsem, d_send, d_recv, f_send, f_recv, p_send, p_recv,
            t_send, t_recv, z_send, z_recv):
     me, w = lax.axis_index("ep"), lax.axis_index("wr")
     zm, pm = me // 4, me % 4
-    tokens, top = ids_ref.shape
+    top, tokens = ids_ref.shape
     pairs, part = hidden_ref.shape
     group = 4 * rows
     width = out_ref.shape[1]
 
+    fetch = pltpu.make_async_copy(hidden_hbm, hidden_ref, hsem)
+    fetch.start()
     load = pltpu.make_async_copy(weight_hbm, weight, wsem)
     load.start()
 
@@ -58,15 +61,33 @@
                     device_id={"ep": partner(zm, j) * 4 + partner(pm, q), "wr": w})
     pl.semaphore_signal(barrier, inc=1, device_id_type=MESH, device_id={"ep": me, "wr": 1 - w})
 
-    flat = flat_ref[...]
-    named = onehot(flat == iota((16, pairs), 0))
-    earlier = onehot(iota((pairs, pairs), 0) < iota((pairs, pairs), 1))
-    slot = jnp.sum(mm(named, earlier) * named.astype(jnp.float32), axis=0, keepdims=True)
-    target = flat * rows + slot.astype(jnp.int32)
+    ids, score = ids_ref[...], score_ref[...]
+    expert_row = iota((16, tokens), 0)
+    hits = [ids[k:k + 1] == expert_row for k in range(top)]
+    scores = jnp.zeros((16, tokens), jnp.float32)
+    for k in range(top):
+        scores = scores + jnp.where(hits[k], score[k:k + 1].astype(jnp.float32), 0.0)
+    before = mm(onehot(scores > 0), onehot(iota((tokens, tokens), 0) < iota((tokens, tokens), 1)))
+    choice = iota((top, tokens), 0)
+    slots = jnp.zeros((top, tokens), jnp.float32)
+    for k in range(top):
+        slot = jnp.sum(jnp.where(hits[k], before, 0.0), axis=0, keepdims=True)
+        slots = slots + jnp.where(choice == k, slot, 0.0)
+
+    first = top * iota((tokens, pairs), 0)
+    pair = iota((tokens, pairs), 1)
+    copies = onehot((pair >= first) & (pair < first + top))
+    turn = (lax.rem(iota((top, pairs), 1), top) == iota((top, pairs), 0)).astype(jnp.float32)
+
+    def by_pair(values):
+        return jnp.sum(mm(values.astype(jnp.bfloat16), copies) * turn, axis=0, keepdims=True)
+
+    target = (by_pair(ids.astype(jnp.float32)) * rows + by_pair(slots)).astype(jnp.int32)
 
     def block(ref, j, p):
         return ref.at[j, pl.ds(pl.multiple_of(p * rows, 16), rows)]
 
+    fetch.wait()
     pl.semaphore_wait(barrier, 16)
 
     dispatch = {}
@@ -88,22 +109,12 @@
             copy.start()
             dispatch[j, q] = copy
 
-    ids, score = ids_ref[...], score_ref[...]
-    lane = iota((tokens, 16), 1)
-    scores = jnp.zeros((tokens, 16), jnp.float32)
-    for k in range(top):
-        scores = scores + jnp.where(
-            ids[:, k:k + 1] == lane, score[:, k:k + 1].astype(jnp.float32), 0.0)
-    gates = 2.827 * scores / jnp.sum(scores, axis=1, keepdims=True)
-    before = mm(onehot(iota((tokens, tokens), 1) < iota((tokens, tokens), 0)), onehot(scores > 0))
-    place = jnp.where(scores > 0, before, EMPTY).astype(jnp.bfloat16)
-    high = gates.astype(jnp.bfloat16)
-    low = (gates - high.astype(jnp.float32)).astype(jnp.bfloat16)
-
-    def put(values, shift):
-        return mm(values, onehot(iota((16, 128), 0) + shift == iota((16, 128), 1)))
-
-    table[0] = (put(place, 0) + put(high, 16) + put(low, 32)).astype(jnp.bfloat16)
+    gates = 2.827 * scores / jnp.sum(scores, axis=0, keepdims=True)
+    place = jnp.where(scores > 0, before, EMPTY)
+    high = gates.astype(jnp.bfloat16).astype(jnp.float32)
+    stacked = jnp.concatenate(
+        [place, high, gates - high, jnp.zeros((80, tokens), jnp.float32)], axis=0)
+    table[0] = stacked.T.astype(jnp.bfloat16)
     tables = {}
     for j in range(1, 4):
         tables[j] = pltpu.make_async_remote_copy(
@@ -124,26 +135,35 @@
             device_id={"ep": me, "wr": 1 - w}, device_id_type=MESH)
         forwards[j].start()
 
-    def expert(j):
-        forwards[j].wait_recv()
-
-        @pl.loop(0, width // TILE)
+    cut = (width // TILE + 1) // 2 * TILE
+    chunks = ((0, cut), (cut, width))
+
+    def tiles(c, body):
+        low, high = chunks[c]
+
+        @pl.loop(low // TILE, high // TILE)
         def _(i):
-            cols = pl.ds(pl.multiple_of(i * TILE, TILE), TILE)
+            body(pl.ds(pl.multiple_of(i * TILE, TILE), TILE))
+
+    def expert(j, c):
+        def body(cols):
             total = mm(arrived[0, j], weight[:part, cols]) + mm(arrived[1, j], weight[part:, cols])
             result[j, :, cols] = total.astype(jnp.bfloat16)
 
-        for q in range(1, 4):
+        tiles(c, body)
+        chunk = pl.ds(chunks[c][0], chunks[c][1] - chunks[c][0])
+        mine = pl.ds(pl.multiple_of(pm * rows, 16), rows)
+        for q in (3, 1, 2):
             pd = partner(pm, q)
-            planars[j, q] = pltpu.make_async_remote_copy(
-                src_ref=block(result, j, pd), dst_ref=block(planar, j, pm),
-                send_sem=p_send.at[j, q], recv_sem=p_recv.at[j, q],
+            theirs = pl.ds(pl.multiple_of(pd * rows, 16), rows)
+            planars[j, q, c] = pltpu.make_async_remote_copy(
+                src_ref=result.at[j, theirs, chunk], dst_ref=planar.at[j, mine, chunk],
+                send_sem=p_send.at[j, q, c], recv_sem=p_recv.at[j, q, c],
                 device_id={"ep": zm * 4 + pd, "wr": w}, device_id_type=MESH)
-            planars[j, q].start()
-        own = pl.ds(pl.multiple_of(pm * rows, 16), rows)
-        planar[j, own] = result[j, own]
-
-    def combine(j):
+            planars[j, q, c].start()
+        planar[j, mine, chunk] = result[j, mine, chunk]
+
+    def spreads(j):
         if j:
             tables[j].wait_recv()
         info = table[j]
@@ -157,21 +177,22 @@
         wide = iota((tokens, group), 1)
         within = wide - rows * sum((wide >= n * rows).astype(jnp.int32) for n in range(1, 4))
         hit = spread(0) == within.astype(jnp.float32)
-        high = jnp.where(hit, spread(16), 0.0).astype(jnp.bfloat16)
-        low = jnp.where(hit, spread(32), 0.0).astype(jnp.bfloat16)
+        for part_at in (0, 1):
+            values = jnp.where(hit, spread(16 + 16 * part_at), 0.0)
+            mixer[j, part_at] = values.astype(jnp.bfloat16)
+
+    def combine(j, c):
         for q in range(1, 4):
-            planars[j, q].wait_recv()
+            planars[j, q, c].wait_recv()
         if j == 2:
-            zcopies[3].wait_recv()
+            zcopies[3, c].wait_recv()
         if j == 0:
-            zcopies[1].wait_recv()
-            zcopies[2].wait_recv()
-
-        @pl.loop(0, width // TILE)
-        def _(i):
-            cols = pl.ds(pl.multiple_of(i * TILE, TILE), TILE)
+            zcopies[1, c].wait_recv()
+            zcopies[2, c].wait_recv()
+
+        def body(cols):
             values = planar[j, :, cols]
-            total = mm(high, values) + mm(low, values)
+            total = mm(mixer[j, 0], values) + mm(mixer[j, 1], values)
             if j == 2:
                 total = total + zrecv[3, :, cols].astype(jnp.float32)
             if j == 0:
@@ -181,21 +202,28 @@
             else:
                 zsend[j, :, cols] = total.astype(jnp.bfloat16)
 
+        tiles(c, body)
         if j:
-            zcopies[j] = pltpu.make_async_remote_copy(
-                src_ref=zsend.at[j], dst_ref=zrecv.at[j],
-                send_sem=z_send.at[j], recv_sem=z_recv.at[j],
+            chunk = pl.ds(chunks[c][0], chunks[c][1] - chunks[c][0])
+            zcopies[j, c] = pltpu.make_async_remote_copy(
+                src_ref=zsend.at[j, :, chunk], dst_ref=zrecv.at[j, :, chunk],
+                send_sem=z_send.at[j, c], recv_sem=z_recv.at[j, c],
                 device_id={"ep": partner(zm, 2 if j == 2 else 1) * 4 + pm, "wr": w},
                 device_id_type=MESH)
-            zcopies[j].start()
+            zcopies[j, c].start()
 
     load.wait()
-    for n, j in enumerate(ORDER):
-        forward(j)
-        expert(j)
-        if n:
-            combine(ORDER[n - 1])
-    combine(ORDER[-1])
+    items = [(j, c) for j in ORDER for c in (0, 1)]
+    for n, (j, c) in enumerate(items):
+        if c == 0:
+            forward(j)
+            spreads(j)
+            forwards[j].wait_recv()
+        expert(j, c)
+        if n >= LAG:
+            combine(*items[n - LAG])
+    for item in items[-LAG:]:
+        combine(*item)
 
     for copies in (dispatch, tables, forwards, planars, zcopies):
         for copy in copies.values():
@@ -214,25 +242,27 @@
     return pl.pallas_call(
         functools.partial(kernel, rows),
         out_shape=jax.ShapeDtypeStruct((tokens, width), bf16),
-        in_specs=[vmem, vmem, vmem, vmem, pl.BlockSpec(memory_space=pl.ANY)],
+        in_specs=[vmem, vmem, pl.BlockSpec(memory_space=pl.ANY), pl.BlockSpec(memory_space=pl.ANY)],
         out_specs=vmem,
         scratch_shapes=[
+            pltpu.VMEM((pairs, part), bf16),
             pltpu.VMEM((full, width), bf16),
             pltpu.VMEM((4, group, part), bf16),
             pltpu.VMEM((2, 4, group, part), bf16),
             pltpu.VMEM((4, group, width), bf16),
             pltpu.VMEM((4, group, width), bf16),
             pltpu.VMEM((4, tokens, 128), bf16),
+            pltpu.VMEM((4, 2, tokens, group), bf16),
             pltpu.VMEM((4, tokens, width), bf16),
             pltpu.VMEM((4, tokens, width), bf16),
-            dma, dma((4, 4)), dma((4, 4)), dma((4,)), dma((4,)), dma((4, 4)), dma((4, 4)),
-            dma((4,)), dma((4,)), dma((4,)), dma((4,)),
+            dma, dma, dma((4, 4)), dma((4, 4)), dma((4,)), dma((4,)), dma((4, 4, 2)), dma((4, 4, 2)),
+            dma((4,)), dma((4,)), dma((4, 2)), dma((4, 2)),
         ],
         compiler_params=pltpu.CompilerParams(
             collective_id=0, has_side_effects=True, vmem_limit_bytes=50 * 1024 * 1024),
         cost_estimate=pl.CostEstimate(
             flops=2 * 16 * rows * full * width, bytes_accessed=2 * full * width, transcendentals=0),
-    )(expert_ids, gate_score, expert_ids.reshape(1, pairs), hidden.reshape(pairs, part), weight[0])
+    )(expert_ids.T, gate_score.T, hidden.reshape(pairs, part), weight[0])
 
 
 def mixing(gate_score):

time: 95.8 us -> 89.1 us (0.930)
  the two profiles are of different devices: /device:TPU:0 before, /device:TPU:27 now
where the time goes in v2:
time: 89.1 us; the launch traced here: 88.8 us
  Pallas kernels  85.5 us (96%)
  local copies, waits for them, and re-layouts  3.37 us (4%)
    pallas_call x1, Pallas kernels, by_kernel(): pl.pallas_call(functools.partial(kernel, rows), out_shape=jax.ShapeDtypeS...  85.5 us
    unnamed x7, local copies, waits for them, and re-layouts  3.37 us

profile of v2, /device:TPU:27, one launch (start us, length us, event | category | flops | bytes accessed | tf_op | source)
XLA Modules:
  0.0 88.8 jit_solution(3449519224542404282)
XLA Ops:
  0.0 0.0 copy-start
  0.0 1.2 %copy-done = bf16[128,8,512]{2,1,0:T(8,128)(2,1)S(1)} copy-done((bf16[128,8,512]{2,1,0:T(8,128)(2,1)S(1)}, bf16[128,8,512]{2,1,0:T(8,128)(2,1)}, u32[]{:S(2)}) %copy-start) | copy-done | bytes 1048600
  1.2 0.0 copy-start.1
  1.2 0.7 copy-done.1
  1.9 0.0 copy-start.2
  1.9 0.7 copy-done.2
  2.6 85.5 %shard_map.46 = bf16[128,1792]{1,0:T(8,128)(2,1)S(1)} custom-call(s32[8,128]{1,0:T(8,128)S(1)} %bitcast.5, s32[8,128]{1,0:T(8,128)S(1)} %bitcast.6, bf16[1024,512]{1,0:T(8,128)(2,1)S(1)} %bitcast.4, bf16[1024,1792]{1,0:T(8,128)(2,1)} %bitcast.7), custom_call_target="tpu_custom_call" | custom-call | flops 4697620480 | bytes 3670016 | tf_op jit(solution)/shard_map/pallas_call | solution.py:242
  88.1 0.8 copy.6
Async XLA Ops:
  0.0 1.2 %copy-start = (bf16[128,8,512]{2,1,0:T(8,128)(2,1)S(1)}, bf16[128,8,512]{2,1,0:T(8,128)(2,1)}, u32[]{:S(2)}) copy-start(bf16[128,8,512]{2,1,0:T(8,128)(2,1)} %param.4) | copy-start | bytes 3145732
  1.2 0.7 copy-start.1
  1.9 0.7 copy-start.2

commit v3 on v2

--- a/solution.py
+++ b/solution.py
@@ -9,7 +9,8 @@
 
 MESH = pl.DeviceIdType.MESH
 ORDER = (1, 3, 2, 0)
-LAG = 2
+LAG = 3
+PARTS = 3
 EMPTY = 255.0
 TILE = 256
 
@@ -95,7 +96,7 @@
         zd = partner(zm, j)
         pick = onehot(target - zd * group == iota((group, pairs), 0))
         outgoing[j] = mm(pick, hidden_ref[...]).astype(jnp.bfloat16)
-        for q in range(4):
+        for q in (3, 2, 1, 0):
             pd = partner(pm, q)
             if j == 0 and q == 0:
                 arrived[w, 0, pl.ds(pl.multiple_of(pm * rows, 16), rows)] = (
@@ -135,8 +136,8 @@
             device_id={"ep": me, "wr": 1 - w}, device_id_type=MESH)
         forwards[j].start()
 
-    cut = (width // TILE + 1) // 2 * TILE
-    chunks = ((0, cut), (cut, width))
+    cuts = [width // TILE * n // PARTS * TILE for n in range(PARTS + 1)]
+    chunks = list(zip(cuts[:-1], cuts[1:]))
 
     def tiles(c, body):
         low, high = chunks[c]
@@ -153,7 +154,7 @@
         tiles(c, body)
         chunk = pl.ds(chunks[c][0], chunks[c][1] - chunks[c][0])
         mine = pl.ds(pl.multiple_of(pm * rows, 16), rows)
-        for q in (3, 1, 2):
+        for q in (1, 2, 3):
             pd = partner(pm, q)
             theirs = pl.ds(pl.multiple_of(pd * rows, 16), rows)
             planars[j, q, c] = pltpu.make_async_remote_copy(
@@ -213,7 +214,7 @@
             zcopies[j, c].start()
 
     load.wait()
-    items = [(j, c) for j in ORDER for c in (0, 1)]
+    items = [(j, c) for j in ORDER for c in range(PARTS)]
     for n, (j, c) in enumerate(items):
         if c == 0:
             forward(j)
@@ -255,8 +256,8 @@
             pltpu.VMEM((4, 2, tokens, group), bf16),
             pltpu.VMEM((4, tokens, width), bf16),
             pltpu.VMEM((4, tokens, width), bf16),
-            dma, dma, dma((4, 4)), dma((4, 4)), dma((4,)), dma((4,)), dma((4, 4, 2)), dma((4, 4, 2)),
-            dma((4,)), dma((4,)), dma((4, 2)), dma((4, 2)),
+            dma, dma, dma((4, 4)), dma((4, 4)), dma((4,)), dma((4,)), dma((4, 4, PARTS)), dma((4, 4, PARTS)),
+            dma((4,)), dma((4,)), dma((4, PARTS)), dma((4, PARTS)),
         ],
         compiler_params=pltpu.CompilerParams(
             collective_id=0, has_side_effects=True, vmem_limit_bytes=50 * 1024 * 1024),

time: 89.1 us -> 87.5 us (0.982)
  the two profiles are of different devices: /device:TPU:27 before, /device:TPU:14 now
where the time goes in v3:
time: 87.5 us; the launch traced here: 87.3 us
  Pallas kernels  83.9 us (96%)
  local copies, waits for them, and re-layouts  3.37 us (4%)
    pallas_call x1, Pallas kernels, by_kernel(): pl.pallas_call(functools.partial(kernel, rows), out_shape=jax.ShapeDtypeS...  83.9 us
    unnamed x7, local copies, waits for them, and re-layouts  3.37 us

profile of v3, /device:TPU:14, one launch (start us, length us, event | category | flops | bytes accessed | tf_op | source)
XLA Modules:
  0.0 87.3 jit_solution(12369530922630327692)
XLA Ops:
  0.0 0.0 copy-start
  0.0 1.2 %copy-done = bf16[128,8,512]{2,1,0:T(8,128)(2,1)S(1)} copy-done((bf16[128,8,512]{2,1,0:T(8,128)(2,1)S(1)}, bf16[128,8,512]{2,1,0:T(8,128)(2,1)}, u32[]{:S(2)}) %copy-start) | copy-done | bytes 1048600
  1.2 0.0 copy-start.1
  1.2 0.7 copy-done.1
  1.9 0.0 copy-start.2
  1.9 0.7 copy-done.2
  2.6 83.9 %shard_map.46 = bf16[128,1792]{1,0:T(8,128)(2,1)S(1)} custom-call(s32[8,128]{1,0:T(8,128)S(1)} %bitcast.5, s32[8,128]{1,0:T(8,128)S(1)} %bitcast.6, bf16[1024,512]{1,0:T(8,128)(2,1)S(1)} %bitcast.4, bf16[1024,1792]{1,0:T(8,128)(2,1)} %bitcast.7), custom_call_target="tpu_custom_call" | custom-call | flops 4697620480 | bytes 3670016 | tf_op jit(solution)/shard_map/pallas_call | solution.py:243
  86.5 0.8 copy.6
Async XLA Ops:
  0.0 1.2 %copy-start = (bf16[128,8,512]{2,1,0:T(8,128)(2,1)S(1)}, bf16[128,8,512]{2,1,0:T(8,128)(2,1)}, u32[]{:S(2)}) copy-start(bf16[128,8,512]{2,1,0:T(8,128)(2,1)} %param.4) | copy-start | bytes 3145732
  1.2 0.7 copy-start.1
  1.9 0.7 copy-start.2

commit v4 on v3

--- a/solution.py
+++ b/solution.py
@@ -217,7 +217,10 @@
     items = [(j, c) for j in ORDER for c in range(PARTS)]
     for n, (j, c) in enumerate(items):
         if c == 0:
-            forward(j)
+            if j == 2:
+                forward(0)
+            if j:
+                forward(j)
             spreads(j)
             forwards[j].wait_recv()
         expert(j, c)

time: 87.5 us -> 87.5 us (level)
  no operation moved by 1% of the time
where the time goes in v4:
time: 87.5 us; the launch traced here: 87.3 us
  Pallas kernels  83.9 us (96%)
  local copies, waits for them, and re-layouts  3.37 us (4%)
    pallas_call x1, Pallas kernels, by_kernel(): pl.pallas_call(functools.partial(kernel, rows), out_shape=jax.ShapeDtypeS...  83.9 us
    unnamed x7, local copies, waits for them, and re-layouts  3.37 us

profile of v4, /device:TPU:14, one launch (start us, length us, event | category | flops | bytes accessed | tf_op | source)
XLA Modules:
  0.0 87.3 jit_solution(11724200088402421537)
XLA Ops:
  0.0 0.0 copy-start
  0.0 1.2 %copy-done = bf16[128,8,512]{2,1,0:T(8,128)(2,1)S(1)} copy-done((bf16[128,8,512]{2,1,0:T(8,128)(2,1)S(1)}, bf16[128,8,512]{2,1,0:T(8,128)(2,1)}, u32[]{:S(2)}) %copy-start) | copy-done | bytes 1048600
  1.2 0.0 copy-start.1
  1.2 0.7 copy-done.1
  1.9 0.0 copy-start.2
  1.9 0.7 copy-done.2
  2.6 83.9 %shard_map.46 = bf16[128,1792]{1,0:T(8,128)(2,1)S(1)} custom-call(s32[8,128]{1,0:T(8,128)S(1)} %bitcast.5, s32[8,128]{1,0:T(8,128)S(1)} %bitcast.6, bf16[1024,512]{1,0:T(8,128)(2,1)S(1)} %bitcast.4, bf16[1024,1792]{1,0:T(8,128)(2,1)} %bitcast.7), custom_call_target="tpu_custom_call" | custom-call | flops 4697620480 | bytes 3670016 | tf_op jit(solution)/shard_map/pallas_call | solution.py:246
  86.5 0.8 copy.6
Async XLA Ops:
  0.0 1.2 %copy-start = (bf16[128,8,512]{2,1,0:T(8,128)(2,1)S(1)}, bf16[128,8,512]{2,1,0:T(8,128)(2,1)}, u32[]{:S(2)}) copy-start(bf16[128,8,512]{2,1,0:T(8,128)(2,1)} %param.4) | copy-start | bytes 3145732
  1.2 0.7 copy-start.1
  1.9 0.7 copy-start.2
